TPU v7x, 32 devices: a whole 2x2x4 slice. The times are simulated.
32 devices in a mesh: dp: 8 (over z, x), fly: 4 (over y, core).
Axes of the slice: x: 2, y: 2, z: 4, core: 2. Of those that a mesh axis runs over, the one named last changes fastest.
Arguments:
- tokens: bfloat16 [1024, 8192], P('dp', 'fly'), may hold values from -6 to 6
- hidden_grad: bfloat16 [1024, 16384], P('dp', 'fly'), may hold values from -6 to 6
- w_up: bfloat16 [6, 256, 16384], P(None, 'dp', 'fly'), may hold values from -0.15625 to 0.15625
- pattern: int32 [6, 64], P(None, 'fly'), may hold values 0 or 1
Outputs:
- input_grad: bfloat16 [1024, 8192], P('dp', 'fly')
- weight_grad: float32 [6, 256, 16384], P(None, 'dp', 'fly')
Inputs may be any that keep to these rules, and one draw needn't show every extreme that they name: pattern[t, f] is 1 where block f of factor t is kept and 0 where it is dropped.
All inputs are finite; a program needn't handle non-finite values.
Results may differ from a plain program's by a relative error of at most 0.0049.
Values may be sent and summed in bfloat16 or wider, within the bound.
A program may use at most 128 MiB of HBM per device.

v0:
```python
import jax
import jax.numpy as jnp
from jax import lax
from jax.sharding import PartitionSpec as P

BS = 256


def partner_2(block, axis, bit):
    count = lax.axis_size(axis)
    route = []
    for low in range(count):
        high = low | 1 << bit
        if high != low and high < count:
            route += [(low, high), (high, low)]
    return lax.ppermute(block, axis, route)


def shifted(value, axis, by):
    devices = lax.axis_size(axis)
    return lax.ppermute(value, axis, [(i, (i + by) % devices) for i in range(devices)])


def flip_blocks(values, stride):
    if stride == 0:
        return values
    row_count, block_count, inner_size = values.shape
    shaped = values.reshape(row_count, block_count // (2 * stride), 2, stride, inner_size)
    return shaped[:, :, ::-1].reshape(row_count, block_count, inner_size)


def stride_of(factor):
    return 0 if factor == 0 else 2 ** (factor - 1)


def pick_rows(stacked, index, replicas):
    return lax.dynamic_index_in_dim(stacked, index % replicas, 1, keepdims=False)


def body(tokens, hidden_grad, w_up, pattern):
    row_count, local_width = tokens.shape
    factor_count = w_up.shape[0]
    hidden_width = hidden_grad.shape[1]
    local_blocks = local_width // BS
    group_width = hidden_width // local_blocks
    weights = lax.all_gather(w_up, "dp", axis=1, tiled=True)
    keep_cols = jnp.broadcast_to(pattern[:, :, None], (factor_count, pattern.shape[1], BS)).reshape(
        factor_count, hidden_width
    )
    masked = (weights * keep_cols.astype(jnp.bfloat16)[:, None, :]).reshape(
        factor_count, BS, local_blocks, group_width
    )
    keep_f = keep_cols.astype(jnp.float32)
    token_blocks = tokens.reshape(row_count, local_blocks, BS)
    gathered = []
    for factor in range(factor_count):
        stride = stride_of(factor)
        if stride < local_blocks:
            gathered.append(flip_blocks(token_blocks, stride))
        else:
            bit_number = (stride // local_blocks).bit_length() - 1
            partner = partner_2(tokens, "fly", bit_number)
            gathered.append(partner.reshape(row_count, local_blocks, BS))
    pre_act = jnp.zeros((row_count, local_blocks, group_width), jnp.float32)
    for factor in range(factor_count):
        pre_act = pre_act + jnp.einsum(
            "ngb,bgc->ngc", gathered[factor], masked[factor], preferred_element_type=jnp.float32
        )
    squash = jax.nn.sigmoid(pre_act)
    derivative = squash * (1.0 + pre_act * (1.0 - squash))
    grad_pre = (
        hidden_grad.reshape(row_count, local_blocks, group_width).astype(jnp.float32) * derivative
    ).astype(jnp.bfloat16)
    input_total = jnp.zeros((row_count, local_blocks, BS), jnp.float32)
    for factor in range(factor_count):
        stride = stride_of(factor)
        contrib = jnp.einsum(
            "ngc,bgc->ngb", grad_pre, masked[factor], preferred_element_type=jnp.float32
        )
        if stride < local_blocks:
            input_total = input_total + flip_blocks(contrib, stride)
        else:
            bit_number = (stride // local_blocks).bit_length() - 1
            returned = partner_2(contrib.reshape(row_count, local_width), "fly", bit_number)
            input_total = input_total + returned.reshape(row_count, local_blocks, BS)
    input_grad = input_total.reshape(row_count, local_width).astype(jnp.bfloat16)
    replicas = lax.axis_size("dp")
    place = lax.axis_index("dp")
    row_share = BS // replicas
    terms = []
    for factor in range(factor_count):
        product_term = jnp.einsum(
            "ngb,ngc->bgc", gathered[factor], grad_pre, preferred_element_type=jnp.float32
        )
        terms.append(product_term.reshape(BS, hidden_width) * keep_f[factor][None, :])
    term_stack = jnp.stack(terms).reshape(factor_count, replicas, row_share, hidden_width)

    def turn_one(step, carry):
        return shifted(carry, "dp", 1) + pick_rows(
            term_stack, place - step - 2 + 2 * replicas, replicas
        )

    summed = lax.fori_loop(
        0, replicas - 1, turn_one, pick_rows(term_stack, place - 1 + replicas, replicas)
    )
    weight_grad = summed * (1.0 / replicas)
    return (input_grad, weight_grad)


def solution(mesh):
    return jax.shard_map(
        body,
        mesh=mesh,
        in_specs=(P("dp", "fly"), P("dp", "fly"), P(None, "dp", "fly"), P(None, "fly")),
        out_specs=(P("dp", "fly"), P(None, "dp", "fly")),
        check_vma=False,
    )
```

profile of v0, /device:TPU:0, one launch (start us, length us, event | category | flops | bytes accessed | tf_op | source)
XLA Modules:
  0.0 891.5 jit_solution(9998804802498803019)
XLA Ops:
  7.9 2.0 copy.47
  10.4 2.5 collective-permute-start.2
  14.2 2.6 copy.38
  18.4 2.8 rev.18
  22.4 167.0 %all-gather.2.cloned.1.call-done = bf16[6,256,4096]{2,1,0:T(8,128)(2,1)} async-done(((bf16[6,32,4096]{2,1,0:T(8,128)(2,1)}), bf16[6,256,4096]{2,1,0:T(8,128)(2,1)}) %all-gather.2.cloned.1.call-update) | async-done | bytes 12582928 | tf_op jit(solution)/shard_map/all_gather | solution.py:46
  189.4 6.1 broadcast_multiply_fusion
  195.5 4.1 fusion.15
  199.5 4.1 copy.49
  203.6 4.1 copy.46
  207.7 4.1 copy.44
  211.8 2.5 copy.42
  214.3 3.3 copy.37
  217.5 4.1 copy.40
  221.6 2.5 fusion.20
  230.5 2.3 fusion.6
  232.7 1.8 fusion.25
  234.5 1.8 fusion.23
  236.3 1.8 fusion.22
  238.1 1.8 fusion.21
  240.0 1.8 fusion.24
  241.8 2.7 convolution_bitcast_fusion.5
  244.5 2.7 convolution_bitcast_fusion.4
  247.2 2.6 convolution_bitcast_fusion.3
  249.8 2.7 convolution_bitcast_fusion.2
  252.5 3.8 convolution_bitcast_fusion.1
  256.3 3.7 convolution_bitcast_fusion
  261.5 2.3 rev.23
  263.7 2.3 rev.22
  266.0 2.3 rev.21
  268.3 5.6 copy.65
  273.8 5.0 reshape.264
  278.8 5.6 copy.66
  284.4 5.0 reshape.265
  289.4 5.6 copy.67
  295.0 4.9 reshape.266
  299.9 5.6 copy.68
  305.5 5.0 reshape.267
  310.4 5.6 copy.70
  316.0 5.0 reshape.268
  321.0 5.6 copy.72
  326.6 5.0 reshape.269
  331.6 2.8 multiply_dynamic-update-slice_fusion.5
  335.6 1.6 copy-done.8
  340.0 1.6 copy-done.10
  344.4 1.9 dynamic-slice_bitcast_fusion
  348.5 1.9 fusion.9
  350.3 4.7 copy-done
  355.1 522.8 %while.17 = (s32[]{:T(128)}, f32[6,32,4096]{2,1,0:T(8,128)}, s32[]{:T(128)}, f32[6,8,32,4096]{3,2,1,0:T(8,128)}, s32[]{:T(128)}, /*index=5*/s32[]{:T(128)}, s32[]{:T(128)}, s32[]{:T(128)}, s32[]{:T(128)}) while((s32[]{:T(128)}, f32[6,32,4096]{2,1,0:T(8,128)}, s32[]{:T(128)}, f32[6,8,32,4096]{3,2,1,0:T(8,128)}, s32[]{:T(128)}, ...), condition=%wide.region_1.2_spmd, body=%wide.region_0.1_spmd.sunk | while | flops 786450 | bytes 22020400 | solution.py:103
  355.6 72.9 %collective-permute-done = f32[6,32,4096]{2,1,0:T(8,128)S(1)} collective-permute-done((f32[6,32,4096]{2,1,0:T(8,128)}, f32[6,32,4096]{2,1,0:T(8,128)S(1)}, u32[]{:S(2)}, u32[]{:S(2)}) %collective-permute-start) | collective-permute-done | bytes 3145760 | tf_op jit(solution)/shard_map/while/body/eval_jaxpr/ppermute | solution.py:21
  428.5 3.9 bitcast_add_fusion.2
  432.4 72.6 %collective-permute-done = f32[6,32,4096]{2,1,0:T(8,128)S(1)} collective-permute-done((f32[6,32,4096]{2,1,0:T(8,128)}, f32[6,32,4096]{2,1,0:T(8,128)S(1)}, u32[]{:S(2)}, u32[]{:S(2)}) %collective-permute-start) | collective-permute-done | bytes 3145760 | tf_op jit(solution)/shard_map/while/body/eval_jaxpr/ppermute | solution.py:21
  505.0 3.9 bitcast_add_fusion.2
  508.9 71.7 %collective-permute-done = f32[6,32,4096]{2,1,0:T(8,128)S(1)} collective-permute-done((f32[6,32,4096]{2,1,0:T(8,128)}, f32[6,32,4096]{2,1,0:T(8,128)S(1)}, u32[]{:S(2)}, u32[]{:S(2)}) %collective-permute-start) | collective-permute-done | bytes 3145760 | tf_op jit(solution)/shard_map/while/body/eval_jaxpr/ppermute | solution.py:21
  580.6 3.9 bitcast_add_fusion.2
  584.5 70.8 %collective-permute-done = f32[6,32,4096]{2,1,0:T(8,128)S(1)} collective-permute-done((f32[6,32,4096]{2,1,0:T(8,128)}, f32[6,32,4096]{2,1,0:T(8,128)S(1)}, u32[]{:S(2)}, u32[]{:S(2)}) %collective-permute-start) | collective-permute-done | bytes 3145760 | tf_op jit(solution)/shard_map/while/body/eval_jaxpr/ppermute | solution.py:21
  655.4 3.9 bitcast_add_fusion.2
  659.3 69.9 %collective-permute-done = f32[6,32,4096]{2,1,0:T(8,128)S(1)} collective-permute-done((f32[6,32,4096]{2,1,0:T(8,128)}, f32[6,32,4096]{2,1,0:T(8,128)S(1)}, u32[]{:S(2)}, u32[]{:S(2)}) %collective-permute-start) | collective-permute-done | bytes 3145760 | tf_op jit(solution)/shard_map/while/body/eval_jaxpr/ppermute | solution.py:21
  729.2 3.9 bitcast_add_fusion.2
  733.0 69.0 %collective-permute-done = f32[6,32,4096]{2,1,0:T(8,128)S(1)} collective-permute-done((f32[6,32,4096]{2,1,0:T(8,128)}, f32[6,32,4096]{2,1,0:T(8,128)S(1)}, u32[]{:S(2)}, u32[]{:S(2)}) %collective-permute-start) | collective-permute-done | bytes 3145760 | tf_op jit(solution)/shard_map/while/body/eval_jaxpr/ppermute | solution.py:21
  802.0 3.9 bitcast_add_fusion.2
  805.9 68.1 %collective-permute-done = f32[6,32,4096]{2,1,0:T(8,128)S(1)} collective-permute-done((f32[6,32,4096]{2,1,0:T(8,128)}, f32[6,32,4096]{2,1,0:T(8,128)S(1)}, u32[]{:S(2)}, u32[]{:S(2)}) %collective-permute-start) | collective-permute-done | bytes 3145760 | tf_op jit(solution)/shard_map/while/body/eval_jaxpr/ppermute | solution.py:21
  874.0 3.9 bitcast_add_fusion.2
  877.9 4.0 broadcast_multiply_fusion.1
  881.9 1.8 add_convert_fusion
  (90 shorter events, 23.4 us)
Async XLA Ops:
  7.2 5.8 copy-start.5
  7.2 182.2 %all-gather.2.cloned.1.call-start = ((), (), s32[]{:S(2)}) async-start(), calls=%async_computation | async-start | bytes 14155776 | tf_op jit(solution)/shard_map/all_gather | solution.py:46
  7.9 6.2 copy-start.22
  10.0 211.7 %collective-permute-start.1 = (bf16[128,2048]{0,1:T(8,128)(2,1)}, bf16[128,2048]{0,1:T(8,128)(2,1)}, u32[]{:S(2)}, u32[]{:S(2)}) collective-permute-start(bf16[128,2048]{0,1:T(8,128)(2,1)} %copy.47), channel_id=1, source_target_pairs={{0,1},{1,0},{2,3},{3,2},{4,5},{5,4},{6,7},{7,6},{8,9},{9,8},{10,11... | collective-permute-start | bytes 1572872 | tf_op jit(solution)/shard_map/ppermute | solution.py:16
  10.4 218.5 %collective-permute-start.2 = (bf16[128,2048]{0,1:T(8,128)(2,1)}, bf16[128,2048]{0,1:T(8,128)(2,1)}, u32[]{:S(2)}, u32[]{:S(2)}) collective-permute-start(bf16[128,2048]{0,1:T(8,128)(2,1)} %copy.47), channel_id=1, source_target_pairs={{0,2},{2,0},{1,3},{3,1},{4,6},{6,4},{5,7},{7,5},{8,10},{10,8},{9,1... | collective-permute-start | bytes 1572872 | tf_op jit(solution)/shard_map/ppermute | solution.py:16
  17.1 207.1 %copy-start.13 = (bf16[128,1,2,4,256]{4,0,3,2,1:T(8,128)(2,1)}, bf16[128,1,2,4,256]{4,0,3,2,1:T(8,128)(2,1)S(1)}, u32[]{:S(2)}) copy-start(bf16[128,1,2,4,256]{4,0,3,2,1:T(8,128)(2,1)S(1)} %copy.45) | copy-start | bytes 1572868
  221.6 2.5 copy-start.2
  224.2 1.6 copy-start.3
  224.2 1.7 copy-start.15
  226.6 1.6 copy-start.4
  226.6 1.7 copy-start.16
  228.2 1.6 copy-start.12
  228.2 2.2 copy-start.21
  238.1 1.8 copy-start.1
  240.0 1.8 copy-start.6
  247.2 2.6 copy-start.14
  260.0 621.8 %collective-permute-start.4 = (f32[128,2048]{0,1:T(8,128)}, f32[128,2048]{0,1:T(8,128)}, u32[]{:S(2)}, u32[]{:S(2)}) collective-permute-start(f32[128,2048]{0,1:T(8,128)} %bitcast.28), channel_id=1, source_target_pairs={{0,2},{2,0},{1,3},{3,1},{4,6},{6,4},{5,7},{7,5},{8,10},{10,8},{9,1... | collective-permute-start | bytes 3145736 | tf_op jit(solution)/shard_map/ppermute | solution.py:16
  268.3 613.6 %collective-permute-start.3 = (f32[128,2048]{0,1:T(8,128)}, f32[128,2048]{0,1:T(8,128)}, u32[]{:S(2)}, u32[]{:S(2)}) collective-permute-start(f32[128,2048]{0,1:T(8,128)} %bitcast.181), channel_id=1, source_target_pairs={{0,1},{1,0},{2,3},{3,2},{4,5},{5,4},{6,7},{7,6},{8,9},{9,8},{10,11... | collective-permute-start | bytes 3145736 | tf_op jit(solution)/shard_map/ppermute | solution.py:16
  331.6 3.4 copy-start.7
  335.0 2.2 copy-start.8
  337.2 2.2 copy-start.9
  339.4 2.2 copy-start.10
  341.6 2.2 copy-start.11
  344.4 10.7 %copy-start = (f32[6,8,32,4096]{3,2,1,0:T(8,128)}, f32[6,8,32,4096]{3,2,1,0:T(8,128)S(1)}, u32[]{:S(2)}) copy-start(f32[6,8,32,4096]{3,2,1,0:T(8,128)S(1)} %multiply_dynamic-update-slice_fusion) | copy-start | bytes 75497472
  344.4 1.9 copy-start.18
  344.4 3.0 copy-start.19
  344.4 4.1 copy-start.20
  355.1 73.4 %collective-permute-start = (f32[6,32,4096]{2,1,0:T(8,128)}, f32[6,32,4096]{2,1,0:T(8,128)S(1)}, u32[]{:S(2)}, u32[]{:S(2)}) collective-permute-start(f32[6,32,4096]{2,1,0:T(8,128)} %get-tuple-element.217), channel_id=1, source_target_pairs={{0,4},{4,8},{8,12},{12,16},{16,20},{20,24},{24,28},{28,0},{1,5},{5... | collective-permute-start | bytes 9437192 | tf_op jit(solution)/shard_map/while/body/eval_jaxpr/ppermute | solution.py:21
  432.4 72.6 %collective-permute-start = (f32[6,32,4096]{2,1,0:T(8,128)}, f32[6,32,4096]{2,1,0:T(8,128)S(1)}, u32[]{:S(2)}, u32[]{:S(2)}) collective-permute-start(f32[6,32,4096]{2,1,0:T(8,128)} %get-tuple-element.217), channel_id=1, source_target_pairs={{0,4},{4,8},{8,12},{12,16},{16,20},{20,24},{24,28},{28,0},{1,5},{5... | collective-permute-start | bytes 9437192 | tf_op jit(solution)/shard_map/while/body/eval_jaxpr/ppermute | solution.py:21
  508.9 71.8 %collective-permute-start = (f32[6,32,4096]{2,1,0:T(8,128)}, f32[6,32,4096]{2,1,0:T(8,128)S(1)}, u32[]{:S(2)}, u32[]{:S(2)}) collective-permute-start(f32[6,32,4096]{2,1,0:T(8,128)} %get-tuple-element.217), channel_id=1, source_target_pairs={{0,4},{4,8},{8,12},{12,16},{16,20},{20,24},{24,28},{28,0},{1,5},{5... | collective-permute-start | bytes 9437192 | tf_op jit(solution)/shard_map/while/body/eval_jaxpr/ppermute | solution.py:21
  584.5 70.8 %collective-permute-start = (f32[6,32,4096]{2,1,0:T(8,128)}, f32[6,32,4096]{2,1,0:T(8,128)S(1)}, u32[]{:S(2)}, u32[]{:S(2)}) collective-permute-start(f32[6,32,4096]{2,1,0:T(8,128)} %get-tuple-element.217), channel_id=1, source_target_pairs={{0,4},{4,8},{8,12},{12,16},{16,20},{20,24},{24,28},{28,0},{1,5},{5... | collective-permute-start | bytes 9437192 | tf_op jit(solution)/shard_map/while/body/eval_jaxpr/ppermute | solution.py:21
  659.2 69.9 %collective-permute-start = (f32[6,32,4096]{2,1,0:T(8,128)}, f32[6,32,4096]{2,1,0:T(8,128)S(1)}, u32[]{:S(2)}, u32[]{:S(2)}) collective-permute-start(f32[6,32,4096]{2,1,0:T(8,128)} %get-tuple-element.217), channel_id=1, source_target_pairs={{0,4},{4,8},{8,12},{12,16},{16,20},{20,24},{24,28},{28,0},{1,5},{5... | collective-permute-start | bytes 9437192 | tf_op jit(solution)/shard_map/while/body/eval_jaxpr/ppermute | solution.py:21
  733.0 69.0 %collective-permute-start = (f32[6,32,4096]{2,1,0:T(8,128)}, f32[6,32,4096]{2,1,0:T(8,128)S(1)}, u32[]{:S(2)}, u32[]{:S(2)}) collective-permute-start(f32[6,32,4096]{2,1,0:T(8,128)} %get-tuple-element.217), channel_id=1, source_target_pairs={{0,4},{4,8},{8,12},{12,16},{16,20},{20,24},{24,28},{28,0},{1,5},{5... | collective-permute-start | bytes 9437192 | tf_op jit(solution)/shard_map/while/body/eval_jaxpr/ppermute | solution.py:21
  805.9 68.1 %collective-permute-start = (f32[6,32,4096]{2,1,0:T(8,128)}, f32[6,32,4096]{2,1,0:T(8,128)S(1)}, u32[]{:S(2)}, u32[]{:S(2)}) collective-permute-start(f32[6,32,4096]{2,1,0:T(8,128)} %get-tuple-element.217), channel_id=1, source_target_pairs={{0,4},{4,8},{8,12},{12,16},{16,20},{20,24},{24,28},{28,0},{1,5},{5... | collective-permute-start | bytes 9437192 | tf_op jit(solution)/shard_map/while/body/eval_jaxpr/ppermute | solution.py:21
  877.9 4.0 copy-start.17
Sparse Core Ops, SparseCore 0:
  10.2 179.1 all-gather.1
where the time goes:
time: 894 us; the launch traced here: 891 us
  waiting for transfers between devices  663 us (74%)
  local copies, waits for them, and re-layouts  128 us (14%)
  other arithmetic  44.8 us (5%)
  matrix products  36.7 us (4%)
  between operations  14.4 us (2%)
    ppermute x7, waiting for transfers between devices, shifted(): lax.ppermute(value, axis, [(i, (i + by) % devices) for i in range(devices)])  495 us
    all_gather x1, waiting for transfers between devices, body(): weights = lax.all_gather(w_up, 'dp', axis=1, tiled=True)  167 us
    transpose x6, local copies, waits for them, and re-layouts, body(): jnp.einsum('ngb,ngc->bgc', gathered[factor], grad_pre, preferred_element_...  33.4 us
    reshape x6, local copies, waits for them, and re-layouts, body(): product_term.reshape(BS, hidden_width) * keep_f[factor][None, :]  29.9 us
    add x7, other arithmetic, turn_one(): shifted(carry, 'dp', 1)  27.2 us
    slice x7, local copies, waits for them, and re-layouts, body(): masked[factor]  26.1 us
    unnamed x59, local copies, waits for them, and re-layouts  20.8 us
    dot_general x6, matrix products, body(): jnp.einsum('ngb,ngc->bgc', gathered[factor], grad_pre, preferred_element_...  18.2 us
  transfers between devices with their start and end apart: 12, of which 8 were waited for; matrix products, arithmetic and copies ran while one was open for 18% of the time, Pallas kernels for 0%

commit v1 on v0

--- a/solution.py
+++ b/solution.py
@@ -37,7 +37,7 @@
     return lax.dynamic_index_in_dim(stacked, index % replicas, 1, keepdims=False)
 
 
-def body(tokens, hidden_grad, w_up, pattern):
+def body_general(tokens, hidden_grad, w_up, pattern):
     row_count, local_width = tokens.shape
     factor_count = w_up.shape[0]
     hidden_width = hidden_grad.shape[1]
@@ -107,6 +107,49 @@
     return (input_grad, weight_grad)
 
 
+def exchanged(value, factor, groups):
+    stride = stride_of(factor)
+    if stride == 0:
+        return value
+    axis, by = ("dp", stride) if stride < groups else ("fly", stride // groups)
+    return lax.ppermute(value, axis, [(i, i ^ by) for i in range(lax.axis_size(axis))])
+
+
+def body_by_group(tokens, hidden_grad, w_up, pattern):
+    groups = lax.axis_size("dp")
+    place = lax.axis_index("dp")
+    factor_count = w_up.shape[0]
+    group_width = hidden_grad.shape[1] // groups
+    own = lax.all_to_all(tokens, "dp", 1, 0, tiled=True)
+    weights = lax.all_to_all(w_up, "dp", 2, 1, tiled=True)
+    upstream = lax.all_to_all(hidden_grad, "dp", 1, 0, tiled=True)
+    per_group = group_width // BS
+    keep = lax.dynamic_slice_in_dim(pattern, place * per_group, per_group, 1)
+    keep_cols = jnp.broadcast_to(keep[:, :, None], keep.shape + (BS,)).reshape(factor_count, 1, group_width)
+    masked = (weights * keep_cols.astype(jnp.bfloat16)).reshape(factor_count * BS, group_width)
+    features = jnp.concatenate([exchanged(own, t, groups) for t in range(factor_count)], axis=1)
+    pre_act = jnp.dot(features, masked, preferred_element_type=jnp.float32)
+    squash = jax.nn.sigmoid(pre_act)
+    derivative = squash * (1.0 + pre_act * (1.0 - squash))
+    grad_pre = (upstream.astype(jnp.float32) * derivative).astype(jnp.bfloat16)
+    contrib = lax.dot_general(grad_pre, masked, (((1,), (1,)), ((), ())), preferred_element_type=jnp.float32)
+    total = contrib[:, :BS]
+    for t in range(1, factor_count):
+        sent = contrib[:, t * BS : (t + 1) * BS].astype(jnp.bfloat16)
+        total = total + exchanged(sent, t, groups).astype(jnp.float32)
+    input_grad = lax.all_to_all(total.astype(jnp.bfloat16), "dp", 0, 1, tiled=True)
+    product = lax.dot_general(features, grad_pre, (((0,), (0,)), ((), ())), preferred_element_type=jnp.float32)
+    product = product.reshape(factor_count, BS, group_width) * (keep_cols.astype(jnp.float32) * (1.0 / groups))
+    weight_grad = lax.all_to_all(product.astype(jnp.bfloat16), "dp", 1, 2, tiled=True)
+    return (input_grad, weight_grad.astype(jnp.float32))
+
+
+def body(tokens, hidden_grad, w_up, pattern):
+    if lax.axis_size("dp") * BS == tokens.shape[1]:
+        return body_by_group(tokens, hidden_grad, w_up, pattern)
+    return body_general(tokens, hidden_grad, w_up, pattern)
+
+
 def solution(mesh):
     return jax.shard_map(
         body,

time: 894 us -> 252 us (0.28)
  waiting for transfers between devices: 663 us -> 150 us
  local copies, waits for them, and re-layouts: 128 us -> 47.8 us
  other arithmetic: 44.8 us -> 5.21 us
  starting transfers between devices: 5.06 us -> 37.2 us
  matrix products: 36.7 us -> 10.1 us
  between operations: 14.4 us -> 0.76 us
    ppermute x11 -> x10, waiting for transfers between devices: 495 us -> 61.2 us  [exchanged(): lax.ppermute(value, axis, [(i, i ^ by) for i in range(lax.axis_size(axis))])]
    all_gather x1 -> x0, waiting for transfers between devices: 167 us -> none  [body(): weights = lax.all_gather(w_up, 'dp', axis=1, tiled=True)]
    all_to_all x0 -> x5, waiting for transfers between devices: none -> 89.3 us  [the longest x1 47.4 us: body_by_group(): lax.all_to_all(product.astype(jnp.bfloat16), 'dp', 1, 2, tiled=True)]
    transpose x6 -> x0, local copies, waits for them, and re-layouts: 33.4 us -> none  [body(): jnp.einsum('ngb,ngc->bgc', gathered[factor], grad_pre, preferred_element_...]
    reshape x6 -> x0, local copies, waits for them, and re-layouts: 29.9 us -> none  [body(): product_term.reshape(BS, hidden_width) * keep_f[factor][None, :]]
    add x7 -> x0, other arithmetic: 27.2 us -> none  [turn_one(): shifted(carry, 'dp', 1)]
    dot_general x18 -> x3, matrix products: 36.7 us -> 10.1 us  [the longest x1 4.52 us: body_by_group(): pre_act = jnp.dot(features, masked, preferred_element_type=jnp.float32)]
    slice x8 -> x1, local copies, waits for them, and re-layouts: 26.1 us -> 0.17 us  [body_by_group(): sent = contrib[:, t * BS:(t + 1) * BS].astype(jnp.bfloat16)]
  transfers between devices with their start and end apart: 12 -> 15, of which waited for: 8 -> 10; matrix products, arithmetic and copies ran while one was open for 18% -> 19% of each run, Pallas kernels for 0% -> 0%
where the time goes in v1:
time: 252 us; the launch traced here: 251 us
  waiting for transfers between devices  150 us (60%)
  local copies, waits for them, and re-layouts  47.8 us (19%)
  starting transfers between devices  37.2 us (15%)
  matrix products  10.1 us (4%)
  other arithmetic  5.21 us (2%)
    ppermute x10, waiting for transfers between devices, exchanged(): lax.ppermute(value, axis, [(i, i ^ by) for i in range(lax.axis_size(axis))])  61.2 us
    all_to_all x1, waiting for transfers between devices, body_by_group(): lax.all_to_all(product.astype(jnp.bfloat16), 'dp', 1, 2, tiled=True)  47.4 us
    all_to_all x1, waiting for transfers between devices, body_by_group(): weights = lax.all_to_all(w_up, 'dp', 2, 1, tiled=True)  34.1 us
    unnamed x17, local copies, waits for them, and re-layouts  31.4 us
    ppermute x10, starting transfers between devices, exchanged(): lax.ppermute(value, axis, [(i, i ^ by) for i in range(lax.axis_size(axis))])  12.3 us
    all_to_all x1, local copies, waits for them, and re-layouts, body_by_group(): weights = lax.all_to_all(w_up, 'dp', 2, 1, tiled=True)  7.76 us
    all_to_all x1, waiting for transfers between devices, body_by_group(): lax.all_to_all(total.astype(jnp.bfloat16), 'dp', 0, 1, tiled=True)  7.7 us
    all_to_all x1, starting transfers between devices, body_by_group(): own = lax.all_to_all(tokens, 'dp', 1, 0, tiled=True)  7.25 us
  transfers between devices with their start and end apart: 15, of which 10 were waited for; matrix products, arithmetic and copies ran while one was open for 19% of the time, Pallas kernels for 0%

profile of v1, /device:TPU:0, one launch (start us, length us, event | category | flops | bytes accessed | tf_op | source)
XLA Modules:
  0.0 251.5 jit_solution(6247420346063093420)
XLA Ops:
  0.6 0.0 copy-start
  0.6 2.2 copy.19
  2.8 7.3 %all-to-all-start.1 = ((bf16[128,8,256]{0,2,1:T(8,128)(2,1)}), bf16[128,8,256]{0,2,1:T(8,128)(2,1)S(1)}, u32[]{:S(2)}, u32[]{:S(2)}) async-start(bf16[128,8,256]{0,2,1:T(8,128)(2,1)} %bitcast.2), calls=%async_computation.1 | async-start | bytes 1048576 | tf_op jit(solution)/shard_map/all_to_all | solution.py:123
  10.1 0.0 copy-done
  10.1 7.3 %copy.21 = bf16[6,32,4096]{1,0,2:T(8,128)(2,1)} copy(bf16[6,32,4096]{2,1,0:T(8,128)(2,1)S(1)} %copy-done) | data formatting | bytes 3145728 | tf_op args[2]
  17.4 10.1 %reshape.51 = bf16[8,2,49152]{2,1,0:T(2,128)(2,1)} reshape(bf16[4096,6,32]{2,1,0:T(8,128)(2,1)} %bitcast.47) | data formatting | bytes 3145728
  27.5 0.0 all-to-all-done.1
  27.5 6.0 %all-to-all-start.2 = ((bf16[8,2,49152]{2,1,0:T(2,128)(2,1)}), bf16[8,2,49152]{2,1,0:T(2,128)(2,1)S(1)}, u32[]{:S(2)}, u32[]{:S(2)}) async-start(bf16[8,2,49152]{2,1,0:T(2,128)(2,1)} %reshape.51), calls=%async_computation.2 | async-start | bytes 3145728 | tf_op jit(solution)/shard_map/all_to_all | solution.py:124
  33.4 0.0 copy-start.1
  33.4 2.3 copy.37
  35.8 34.1 %all-to-all-done.2 = bf16[8,2,49152]{2,1,0:T(2,128)(2,1)S(1)} async-done(((bf16[8,2,49152]{2,1,0:T(2,128)(2,1)}), bf16[8,2,49152]{2,1,0:T(2,128)(2,1)S(1)}, u32[]{:S(2)}, u32[]{:S(2)}) %all-to-all-start.2) | async-done | bytes 1572896 | tf_op jit(solution)/shard_map/all_to_all | solution.py:124
  69.9 4.2 %all-to-all-start = ((bf16[128,8,512]{2,0,1:T(8,128)(2,1)}), bf16[128,8,512]{2,0,1:T(8,128)(2,1)}, u32[]{:S(2)}, u32[]{:S(2)}) async-start(bf16[128,8,512]{2,0,1:T(8,128)(2,1)} %bitcast.45), calls=%async_computation | async-start | bytes 2097152 | tf_op jit(solution)/shard_map/all_to_all | solution.py:125
  74.1 0.2 copy.20
  74.3 2.0 collective-permute-start
  76.3 1.5 collective-permute-start.1
  77.8 0.0 copy-done.1
  77.8 0.1 dynamic-slice_convert_fusion
  77.9 0.0 collective-permute-start.3
  77.9 2.5 collective-permute-start.2
  80.3 0.1 broadcast_bitcast_fusion.1
  80.4 1.6 collective-permute-start.4
  82.0 0.8 constant_dynamic-update-slice_fusion.5
  82.8 15.7 %collective-permute-done = bf16[1024,256]{1,0:T(8,128)(2,1)S(1)} collective-permute-done((bf16[1024,256]{1,0:T(8,128)(2,1)S(1)}, bf16[1024,256]{1,0:T(8,128)(2,1)S(1)}, u32[]{:S(2)}, u32[]{:S(2)}) %collective-permute-start) | collective-permute-done | bytes 524320 | tf_op jit(solution)/shard_map/ppermute | solution.py:115
  98.5 0.8 constant_dynamic-update-slice_fusion.4
  99.4 11.3 %collective-permute-done.1 = bf16[1024,256]{1,0:T(8,128)(2,1)S(1)} collective-permute-done((bf16[1024,256]{1,0:T(8,128)(2,1)S(1)}, bf16[1024,256]{1,0:T(8,128)(2,1)S(1)}, u32[]{:S(2)}, u32[]{:S(2)}) %collective-permute-start.1) | collective-permute-done | bytes 524320 | tf_op jit(solution)/shard_map/ppermute | solution.py:115
  110.7 0.8 constant_dynamic-update-slice_fusion.3
  111.5 10.7 %collective-permute-done.2 = bf16[1024,256]{1,0:T(8,128)(2,1)S(1)} collective-permute-done((bf16[1024,256]{1,0:T(8,128)(2,1)S(1)}, bf16[1024,256]{1,0:T(8,128)(2,1)S(1)}, u32[]{:S(2)}, u32[]{:S(2)}) %collective-permute-start.2) | collective-permute-done | bytes 524320 | tf_op jit(solution)/shard_map/ppermute | solution.py:115
  122.2 0.8 constant_dynamic-update-slice_fusion.2
  123.0 0.0 collective-permute-done.3
  123.0 0.8 constant_dynamic-update-slice_fusion.1
  123.8 0.0 collective-permute-done.4
  123.8 0.8 constant_dynamic-update-slice_fusion
  124.7 7.6 %reshape.52 = bf16[4096,6,32]{2,1,0:T(8,128)(2,1)} reshape(bf16[8,2,49152]{2,1,0:T(2,128)(2,1)S(1)} %all-to-all-done.2) | data formatting | bytes 3145728
  132.2 7.8 %copy.23 = bf16[6,8,32,512]{3,2,1,0:T(8,128)(2,1)S(1)} copy(bf16[6,8,32,512]{2,0,3,1:T(8,128)(2,1)} %bitcast.46) | data formatting | bytes 3145728 | tf_op jit(solution)/shard_map/all_to_all | solution.py:124
  140.0 0.2 bitcast_multiply_fusion.1
  140.2 0.0 all-to-all-done
  140.2 4.5 %fusion.1 = bf16[1024,512]{1,0:T(8,128)(2,1)S(1)} fusion(bf16[128,8,512]{2,0,1:T(8,128)(2,1)} %all-to-all-done, bf16[1024,1536]{1,0:T(8,128)(2,1)} %constant_dynamic-update-slice_fusion, bf16[1536,512]{1,0:T(8,128)(2,1)S(1)} %bitcast_multiply_fusion.1), kind=kOutput, calls=%fused_computation.4 | convolution fusion | flops 1615855616 | bytes 6815744 | tf_op jit(solution)/shard_map/dot_general | solution.py:131
  144.7 1.8 fusion.8
  146.6 0.2 fusion.7
  146.7 1.3 collective-permute-start.5
  148.1 1.5 collective-permute-start.9
  149.6 0.0 collective-permute-start.8
  149.6 0.0 collective-permute-start.7
  149.6 2.0 collective-permute-start.6
  151.6 0.1 convert_multiply_fusion
  151.7 7.5 %collective-permute-done.5 = bf16[1024,256]{1,0:T(8,128)(2,1)S(1)} collective-permute-done((bf16[1024,256]{1,0:T(8,128)(2,1)S(1)}, bf16[1024,256]{1,0:T(8,128)(2,1)S(1)}, u32[]{:S(2)}, u32[]{:S(2)}) %collective-permute-start.5) | collective-permute-done | bytes 524320 | tf_op jit(solution)/shard_map/ppermute | solution.py:115
  159.2 1.5 collective-permute-done.9
  160.6 0.0 collective-permute-done.8
  160.6 14.3 %collective-permute-done.7 = bf16[1024,256]{1,0:T(8,128)(2,1)S(1)} collective-permute-done((bf16[1024,256]{1,0:T(8,128)(2,1)S(1)}, bf16[1024,256]{1,0:T(8,128)(2,1)S(1)}, u32[]{:S(2)}, u32[]{:S(2)}) %collective-permute-start.7) | collective-permute-done | bytes 524320 | tf_op jit(solution)/shard_map/ppermute | solution.py:115
  175.0 0.2 collective-permute-done.6
  175.2 1.3 fusion.6
  176.4 3.6 %all-to-all-start.3 = ((bf16[8,128,256]{2,1,0:T(8,128)(2,1)}), bf16[8,128,256]{2,1,0:T(8,128)(2,1)S(1)}, u32[]{:S(2)}, u32[]{:S(2)}) async-start(bf16[8,128,256]{2,1,0:T(8,128)(2,1)} %bitcast.10), calls=%async_computation.3 | async-start | bytes 1048576 | tf_op jit(solution)/shard_map/all_to_all | solution.py:140
  180.1 0.1 broadcast_bitcast_fusion
  180.2 3.8 %fusion.9 = f32[1536,512]{1,0:T(8,128)S(1)} fusion(bf16[1024,1536]{1,0:T(8,128)(2,1)} %constant_dynamic-update-slice_fusion, bf16[1024,512]{1,0:T(8,128)(2,1)S(1)} %fusion.1), kind=kOutput, calls=%fused_computation.25 | convolution fusion | flops 1610612736 | bytes 7340032 | tf_op jit(solution)/shard_map/dot_general | solution.py:141
  183.9 3.0 %fusion = bf16[6,256,512]{2,0,1:T(8,128)(2,1)} fusion(f32[6,256,512]{2,1,0:T(8,128)S(1)} %bitcast.49, f32[6,512]{1,0:T(8,128)S(1)} %bitcast.60), kind=kLoop, calls=%fused_computation.2 | loop fusion | flops 1572864 | bytes 4730880 | tf_op jit(solution)/shard_map/convert_element_type | solution.py:143
  186.9 7.7 %all-to-all-done.3 = bf16[8,128,256]{2,1,0:T(8,128)(2,1)S(1)} async-done(((bf16[8,128,256]{2,1,0:T(8,128)(2,1)}), bf16[8,128,256]{2,1,0:T(8,128)(2,1)S(1)}, u32[]{:S(2)}, u32[]{:S(2)}) %all-to-all-start.3) | async-done | bytes 524320 | tf_op jit(solution)/shard_map/all_to_all | solution.py:140
  194.6 3.8 %all-to-all-start.4 = ((bf16[6,256,512]{2,0,1:T(8,128)(2,1)}), bf16[6,256,512]{2,0,1:T(8,128)(2,1)S(1)}, u32[]{:S(2)}, u32[]{:S(2)}) async-start(bf16[6,256,512]{2,0,1:T(8,128)(2,1)} %fusion), calls=%async_computation.4 | async-start | bytes 4194304 | tf_op jit(solution)/shard_map/all_to_all | solution.py:143
  198.4 0.8 copy.30
  199.3 47.4 %all-to-all-done.4 = bf16[6,256,512]{2,0,1:T(8,128)(2,1)S(1)} async-done(((bf16[6,256,512]{2,0,1:T(8,128)(2,1)}), bf16[6,256,512]{2,0,1:T(8,128)(2,1)S(1)}, u32[]{:S(2)}, u32[]{:S(2)}) %all-to-all-start.4) | async-done | bytes 1572896 | tf_op jit(solution)/shard_map/all_to_all | solution.py:143
  246.7 0.5 convert_bitcast_fusion
  247.3 1.8 copy.26
  249.1 2.3 reshape.49
  (2 shorter events, 0.0 us)
Async XLA Ops:
  0.6 9.4 %copy-start = (bf16[6,32,4096]{2,1,0:T(8,128)(2,1)S(1)}, bf16[6,32,4096]{2,1,0:T(8,128)(2,1)}, u32[]{:S(2)}) copy-start(bf16[6,32,4096]{2,1,0:T(8,128)(2,1)} %param.6) | copy-start | bytes 4718596
  2.8 24.7 %all-to-all-start.1 = ((bf16[128,8,256]{0,2,1:T(8,128)(2,1)}), bf16[128,8,256]{0,2,1:T(8,128)(2,1)S(1)}, u32[]{:S(2)}, u32[]{:S(2)}) async-start(bf16[128,8,256]{0,2,1:T(8,128)(2,1)} %bitcast.2), calls=%async_computation.1 | async-start | bytes 1048576 | tf_op jit(solution)/shard_map/all_to_all | solution.py:123
  27.5 42.4 %all-to-all-start.2 = ((bf16[8,2,49152]{2,1,0:T(2,128)(2,1)}), bf16[8,2,49152]{2,1,0:T(2,128)(2,1)S(1)}, u32[]{:S(2)}, u32[]{:S(2)}) async-start(bf16[8,2,49152]{2,1,0:T(2,128)(2,1)} %reshape.51), calls=%async_computation.2 | async-start | bytes 3145728 | tf_op jit(solution)/shard_map/all_to_all | solution.py:124
  33.4 44.3 %copy-start.1 = (s32[6,16]{1,0:T(8,128)S(1)}, s32[6,16]{1,0:T(8,128)}, u32[]{:S(2)}) copy-start(s32[6,16]{1,0:T(8,128)} %param.7) | copy-start | bytes 1156
  69.9 70.3 %all-to-all-start = ((bf16[128,8,512]{2,0,1:T(8,128)(2,1)}), bf16[128,8,512]{2,0,1:T(8,128)(2,1)}, u32[]{:S(2)}, u32[]{:S(2)}) async-start(bf16[128,8,512]{2,0,1:T(8,128)(2,1)} %bitcast.45), calls=%async_computation | async-start | bytes 2097152 | tf_op jit(solution)/shard_map/all_to_all | solution.py:125
  74.3 24.2 %collective-permute-start = (bf16[1024,256]{1,0:T(8,128)(2,1)S(1)}, bf16[1024,256]{1,0:T(8,128)(2,1)S(1)}, u32[]{:S(2)}, u32[]{:S(2)}) collective-permute-start(bf16[1024,256]{1,0:T(8,128)(2,1)S(1)} %bitcast.50), channel_id=1, source_target_pairs={{0,4},{4,0},{8,12},{12,8},{16,20},{20,16},{24,28},{28,24},{1,5},{5... | collective-permute-start | bytes 1572872 | tf_op jit(solution)/shard_map/ppermute | solution.py:115
  76.3 34.4 %collective-permute-start.1 = (bf16[1024,256]{1,0:T(8,128)(2,1)S(1)}, bf16[1024,256]{1,0:T(8,128)(2,1)S(1)}, u32[]{:S(2)}, u32[]{:S(2)}) collective-permute-start(bf16[1024,256]{1,0:T(8,128)(2,1)S(1)} %bitcast.51), channel_id=1, source_target_pairs={{0,8},{4,12},{8,0},{12,4},{16,24},{20,28},{24,16},{28,20},{1,9},{5... | collective-permute-start | bytes 1572872 | tf_op jit(solution)/shard_map/ppermute | solution.py:115
  77.9 45.1 %collective-permute-start.3 = (bf16[1024,256]{1,0:T(8,128)(2,1)S(1)}, bf16[1024,256]{1,0:T(8,128)(2,1)S(1)}, u32[]{:S(2)}, u32[]{:S(2)}) collective-permute-start(bf16[1024,256]{1,0:T(8,128)(2,1)S(1)} %bitcast.52), channel_id=1, source_target_pairs={{0,1},{1,0},{2,3},{3,2},{4,5},{5,4},{6,7},{7,6},{8,9},{9,8},{10,11... | collective-permute-start | bytes 1572872 | tf_op jit(solution)/shard_map/ppermute | solution.py:115
  77.9 44.3 %collective-permute-start.2 = (bf16[1024,256]{1,0:T(8,128)(2,1)S(1)}, bf16[1024,256]{1,0:T(8,128)(2,1)S(1)}, u32[]{:S(2)}, u32[]{:S(2)}) collective-permute-start(bf16[1024,256]{1,0:T(8,128)(2,1)S(1)} %bitcast.53), channel_id=1, source_target_pairs={{0,16},{4,20},{8,24},{12,28},{16,0},{20,4},{24,8},{28,12},{1,17},{... | collective-permute-start | bytes 1572872 | tf_op jit(solution)/shard_map/ppermute | solution.py:115
  80.4 43.4 %collective-permute-start.4 = (bf16[1024,256]{1,0:T(8,128)(2,1)S(1)}, bf16[1024,256]{1,0:T(8,128)(2,1)S(1)}, u32[]{:S(2)}, u32[]{:S(2)}) collective-permute-start(bf16[1024,256]{1,0:T(8,128)(2,1)S(1)} %bitcast.54), channel_id=1, source_target_pairs={{0,2},{1,3},{2,0},{3,1},{4,6},{5,7},{6,4},{7,5},{8,10},{9,11},{10,... | collective-permute-start | bytes 1572872 | tf_op jit(solution)/shard_map/ppermute | solution.py:115
  146.7 12.4 %collective-permute-start.5 = (bf16[1024,256]{1,0:T(8,128)(2,1)S(1)}, bf16[1024,256]{1,0:T(8,128)(2,1)S(1)}, u32[]{:S(2)}, u32[]{:S(2)}) collective-permute-start(bf16[1024,256]{1,0:T(8,128)(2,1)S(1)} %get-tuple-element.2), channel_id=1, source_target_pairs={{0,4},{4,0},{8,12},{12,8},{16,20},{20,16},{24,28},{28,24},{1,5},{5... | collective-permute-start | bytes 1572872 | tf_op jit(solution)/shard_map/ppermute | solution.py:115
  148.1 12.6 %collective-permute-start.9 = (bf16[1024,256]{1,0:T(8,128)(2,1)S(1)}, bf16[1024,256]{1,0:T(8,128)(2,1)S(1)}, u32[]{:S(2)}, u32[]{:S(2)}) collective-permute-start(bf16[1024,256]{1,0:T(8,128)(2,1)S(1)} %get-tuple-element.3), channel_id=1, source_target_pairs={{0,2},{1,3},{2,0},{3,1},{4,6},{5,7},{6,4},{7,5},{8,10},{9,11},{10,... | collective-permute-start | bytes 1572872 | tf_op jit(solution)/shard_map/ppermute | solution.py:115
  149.6 11.1 %collective-permute-start.8 = (bf16[1024,256]{1,0:T(8,128)(2,1)S(1)}, bf16[1024,256]{1,0:T(8,128)(2,1)S(1)}, u32[]{:S(2)}, u32[]{:S(2)}) collective-permute-start(bf16[1024,256]{1,0:T(8,128)(2,1)S(1)} %get-tuple-element.4), channel_id=1, source_target_pairs={{0,1},{1,0},{2,3},{3,2},{4,5},{5,4},{6,7},{7,6},{8,9},{9,8},{10,11... | collective-permute-start | bytes 1572872 | tf_op jit(solution)/shard_map/ppermute | solution.py:115
  149.6 25.4 %collective-permute-start.7 = (bf16[1024,256]{1,0:T(8,128)(2,1)S(1)}, bf16[1024,256]{1,0:T(8,128)(2,1)S(1)}, u32[]{:S(2)}, u32[]{:S(2)}) collective-permute-start(bf16[1024,256]{1,0:T(8,128)(2,1)S(1)} %get-tuple-element.5), channel_id=1, source_target_pairs={{0,16},{4,20},{8,24},{12,28},{16,0},{20,4},{24,8},{28,12},{1,17},{... | collective-permute-start | bytes 1572872 | tf_op jit(solution)/shard_map/ppermute | solution.py:115
  149.6 25.6 %collective-permute-start.6 = (bf16[1024,256]{1,0:T(8,128)(2,1)S(1)}, bf16[1024,256]{1,0:T(8,128)(2,1)S(1)}, u32[]{:S(2)}, u32[]{:S(2)}) collective-permute-start(bf16[1024,256]{1,0:T(8,128)(2,1)S(1)} %get-tuple-element.6), channel_id=1, source_target_pairs={{0,8},{4,12},{8,0},{12,4},{16,24},{20,28},{24,16},{28,20},{1,9},{5... | collective-permute-start | bytes 1572872 | tf_op jit(solution)/shard_map/ppermute | solution.py:115
  176.4 18.2 %all-to-all-start.3 = ((bf16[8,128,256]{2,1,0:T(8,128)(2,1)}), bf16[8,128,256]{2,1,0:T(8,128)(2,1)S(1)}, u32[]{:S(2)}, u32[]{:S(2)}) async-start(bf16[8,128,256]{2,1,0:T(8,128)(2,1)} %bitcast.10), calls=%async_computation.3 | async-start | bytes 1048576 | tf_op jit(solution)/shard_map/all_to_all | solution.py:140
  194.6 52.1 %all-to-all-start.4 = ((bf16[6,256,512]{2,0,1:T(8,128)(2,1)}), bf16[6,256,512]{2,0,1:T(8,128)(2,1)S(1)}, u32[]{:S(2)}, u32[]{:S(2)}) async-start(bf16[6,256,512]{2,0,1:T(8,128)(2,1)} %fusion), calls=%async_computation.4 | async-start | bytes 4194304 | tf_op jit(solution)/shard_map/all_to_all | solution.py:143

commit v2 on v0

--- a/solution.py
+++ b/solution.py
@@ -1,6 +1,10 @@
+import functools
+
 import jax
 import jax.numpy as jnp
 from jax import lax
+from jax.experimental import pallas as pl
+from jax.experimental.pallas import tpu as pltpu
 from jax.sharding import PartitionSpec as P
 
 BS = 256
@@ -37,7 +41,7 @@
     return lax.dynamic_index_in_dim(stacked, index % replicas, 1, keepdims=False)
 
 
-def body(tokens, hidden_grad, w_up, pattern):
+def body_general(tokens, hidden_grad, w_up, pattern):
     row_count, local_width = tokens.shape
     factor_count = w_up.shape[0]
     hidden_width = hidden_grad.shape[1]
@@ -107,6 +111,264 @@
     return (input_grad, weight_grad)
 
 
+def flipped(index, by, limit):
+    out, bit = 0, 1
+    while bit < limit:
+        differ = lax.rem(lax.div(index, jnp.int32(bit)) + lax.div(by, jnp.int32(bit)), jnp.int32(2))
+        out, bit = out + differ * bit, bit * 2
+    return out
+
+
+def part(index, size):
+    return pl.ds(pl.multiple_of(index * size, size), size)
+
+
+def group_kernel(
+    groups, flies, tokens, hidden_grad, w_up, pattern, sums_out, grads_out,
+    feat, weights, upstream, grad_pre, masked, own_term, near_out, near_in, far_out, home_sum, product,
+    token_send, token_recv, far_send, far_recv, weight_send, weight_recv, up_send, up_recv,
+    pass_send, pass_recv, back_send, back_recv, other_send, other_recv, home_send, home_recv,
+    grad_send, grad_recv, local_sem,
+):
+    me, fly = lax.axis_index("dp"), lax.axis_index("fly")
+    rows = tokens.shape[0]
+    factors, share = w_up.shape[0], w_up.shape[1]
+    width = upstream.shape[1]
+    per_group = width // BS
+    half = groups // 2
+    far = [t for t in range(factors) if stride_of(t) == half][0]
+    near = [t for t in range(1, factors) if t != far]
+
+    def partner(t):
+        stride = stride_of(t)
+        if stride < groups:
+            return {"dp": flipped(me, jnp.int32(stride), groups)}
+        return {"fly": flipped(fly, jnp.int32(stride // groups), flies)}
+
+    def remote(src, dst, send, recv, device):
+        return pltpu.make_async_remote_copy(
+            src_ref=src, dst_ref=dst, send_sem=send, recv_sem=recv, device_id=device,
+            device_id_type=pl.DeviceIdType.MESH,
+        )
+
+    def peer(k):
+        return flipped(me, jnp.int32(k), groups)
+
+    def token_copy(to, at):
+        return remote(tokens.at[:, part(to, BS)], feat.at[0, part(at, rows)], token_send.at[to], token_recv.at[at], {"dp": to})
+
+    def far_copy(to, at):
+        other = flipped(to, jnp.int32(half), groups)
+        return remote(tokens.at[:, part(other, BS)], feat.at[far, part(at, rows)], far_send.at[to], far_recv.at[at], {"dp": to})
+
+    def weight_copy(to, at):
+        return remote(w_up.at[:, :, part(to, width)], weights.at[:, part(at, share)], weight_send.at[to], weight_recv.at[at], {"dp": to})
+
+    def up_copy(to, at):
+        return remote(hidden_grad.at[:, part(to, width)], upstream.at[part(at, rows)], up_send.at[to], up_recv.at[at], {"dp": to})
+
+    def pass_copy(i, s):
+        t = near[i]
+        return remote(feat.at[0, part(s, rows)], feat.at[t, part(s, rows)], pass_send.at[i, s], pass_recv.at[i, s], partner(t))
+
+    def back_copy(i, s):
+        return remote(near_out.at[i, part(s, rows)], near_in.at[i, part(s, rows)], back_send.at[i, s], back_recv.at[i, s], partner(near[i]))
+
+    def other_copy(to, at):
+        block = flipped(at, jnp.int32(half), groups)
+        return remote(far_out.at[part(to, rows)], sums_out.at[1, :, part(block, BS)], other_send.at[to], other_recv.at[at], {"dp": to})
+
+    def home_copy(to, at):
+        return remote(home_sum.at[part(to, rows)], sums_out.at[0, :, part(at, BS)], home_send.at[to], home_recv.at[at], {"dp": to})
+
+    def grad_copy(to, at):
+        return remote(product.at[:, part(to, share)], grads_out.at[:, :, part(at, width)], grad_send.at[to], grad_recv.at[at], {"dp": to})
+
+    barrier = pltpu.get_barrier_semaphore()
+    for k in range(1, groups):
+        pl.semaphore_signal(barrier, inc=1, device_id={"dp": peer(k)}, device_id_type=pl.DeviceIdType.MESH)
+    across = [t for t in near if stride_of(t) >= groups]
+    for t in across:
+        pl.semaphore_signal(barrier, inc=1, device_id=partner(t), device_id_type=pl.DeviceIdType.MESH)
+    pl.semaphore_wait(barrier, groups - 1 + len(across))
+
+    order = list(range(groups - 1, 0, -1))
+    for copy in (token_copy, far_copy, weight_copy, up_copy):
+        for k in order:
+            copy(peer(k), me).start()
+    across_me = flipped(me, jnp.int32(half), groups)
+    local = [
+        pltpu.make_async_copy(tokens.at[:, part(me, BS)], feat.at[0, part(me, rows)], local_sem.at[0]),
+        pltpu.make_async_copy(tokens.at[:, part(across_me, BS)], feat.at[far, part(me, rows)], local_sem.at[1]),
+        pltpu.make_async_copy(w_up.at[:, :, part(me, width)], weights.at[:, part(me, share)], local_sem.at[2]),
+        pltpu.make_async_copy(hidden_grad.at[:, part(me, width)], upstream.at[part(me, rows)], local_sem.at[3]),
+    ]
+    for copy in local:
+        copy.start()
+
+    local[0].wait()
+    for i in range(len(near)):
+        pass_copy(i, me).start()
+
+    def pass_on(k, carry):
+        source = flipped(me, k, groups)
+        token_copy(source, source).wait_recv()
+        for i in range(len(near)):
+            pass_copy(i, source).start()
+        return carry
+
+    lax.fori_loop(1, groups, pass_on, 0)
+
+    place = lax.broadcasted_iota(jnp.int32, pattern.shape, 1)
+    keep = [
+        jnp.sum(jnp.where(place == me * per_group + j, pattern[...], 0).astype(jnp.float32), axis=1, keepdims=True)
+        for j in range(per_group)
+    ]
+    for copy in local[1:]:
+        copy.wait()
+    for k in range(1, groups):
+        weight_copy(peer(k), peer(k)).wait_recv()
+    for t in range(factors):
+        for j in range(per_group):
+            piece = weights[t, :, j * BS : (j + 1) * BS]
+            masked[t * BS : (t + 1) * BS, j * BS : (j + 1) * BS] = piece * keep[j][t : t + 1].astype(jnp.bfloat16)
+
+    def work(source):
+        at = part(source, rows)
+        for i in range(len(near)):
+            pass_copy(i, source).wait_recv()
+        features = jnp.concatenate([feat[t, at, :] for t in range(factors)], axis=1)
+        pre_act = jnp.dot(features, masked[...], preferred_element_type=jnp.float32)
+        squash = jax.nn.sigmoid(pre_act)
+        derivative = squash * (1.0 + pre_act * (1.0 - squash))
+        rounded = (upstream[at, :].astype(jnp.float32) * derivative).astype(jnp.bfloat16)
+        grad_pre[at, :] = rounded
+        contrib = lax.dot_general(rounded, masked[...], (((1,), (1,)), ((), ())), preferred_element_type=jnp.float32)
+        own_term[at, :] = contrib[:, :BS]
+        far_out[at, :] = contrib[:, far * BS : (far + 1) * BS].astype(jnp.bfloat16)
+        for i, t in enumerate(near):
+            near_out[i, at, :] = contrib[:, t * BS : (t + 1) * BS].astype(jnp.bfloat16)
+            back_copy(i, source).start()
+
+    work(me)
+    own_far = pltpu.make_async_copy(far_out.at[part(me, rows)], sums_out.at[1, :, part(across_me, BS)], local_sem.at[1])
+    own_far.start()
+
+    def work_step(k, carry):
+        source = flipped(me, k, groups)
+        far_copy(source, source).wait_recv()
+        up_copy(source, source).wait_recv()
+        work(source)
+        other_copy(source, me).start()
+        return carry
+
+    lax.fori_loop(1, groups, work_step, 0)
+
+    for t in range(factors):
+        term = lax.dot_general(feat[t], grad_pre[...], (((0,), (0,)), ((), ())), preferred_element_type=jnp.float32)
+        for j in range(per_group):
+            scale = keep[j][t : t + 1] * (1.0 / groups)
+            product[t, :, j * BS : (j + 1) * BS] = (term[:, j * BS : (j + 1) * BS] * scale).astype(jnp.bfloat16)
+    for k in order:
+        grad_copy(peer(k), me).start()
+    own_grad = pltpu.make_async_copy(product.at[:, part(me, share)], grads_out.at[:, :, part(me, width)], local_sem.at[2])
+    own_grad.start()
+
+    def add_up(source):
+        at = part(source, rows)
+        total = own_term[at, :]
+        for i in range(len(near)):
+            back_copy(i, source).wait_recv()
+            total = total + near_in[i, at, :].astype(jnp.float32)
+        home_sum[at, :] = total.astype(jnp.bfloat16)
+
+    add_up(me)
+    own_home = pltpu.make_async_copy(home_sum.at[part(me, rows)], sums_out.at[0, :, part(me, BS)], local_sem.at[0])
+    own_home.start()
+
+    def add_step(k, carry):
+        source = flipped(me, k, groups)
+        add_up(source)
+        home_copy(source, me).start()
+        return carry
+
+    lax.fori_loop(1, groups, add_step, 0)
+
+    def finish(k, carry):
+        other = flipped(me, k, groups)
+        for copy in (other_copy, home_copy, grad_copy):
+            copy(other, other).wait_recv()
+        for copy in (token_copy, far_copy, weight_copy, up_copy, other_copy, home_copy, grad_copy):
+            copy(other, me).wait_send()
+        return carry
+
+    lax.fori_loop(1, groups, finish, 0)
+
+    def finish_near(s, carry):
+        for i in range(len(near)):
+            pass_copy(i, s).wait_send()
+            back_copy(i, s).wait_send()
+        return carry
+
+    lax.fori_loop(0, groups, finish_near, 0)
+    own_far.wait()
+    own_home.wait()
+    own_grad.wait()
+
+
+def body_by_group(tokens, hidden_grad, w_up, pattern):
+    groups, flies = lax.axis_size("dp"), lax.axis_size("fly")
+    factors, share = w_up.shape[0], w_up.shape[1]
+    rows = tokens.shape[0]
+    width = hidden_grad.shape[1] // groups
+    every = rows * groups
+    near = factors - 2
+    dma = pltpu.SemaphoreType.DMA
+    bf16, f32 = jnp.bfloat16, jnp.float32
+    anywhere = pl.BlockSpec(memory_space=pl.ANY)
+    flops = 6 * every * factors * BS * width
+    sums, grads = pl.pallas_call(
+        functools.partial(group_kernel, groups, flies),
+        out_shape=(
+            jax.ShapeDtypeStruct((2, rows, groups * BS), bf16),
+            jax.ShapeDtypeStruct((factors, share, groups * width), bf16),
+        ),
+        in_specs=[anywhere, anywhere, anywhere, pl.BlockSpec(memory_space=pltpu.VMEM)],
+        out_specs=(anywhere, anywhere),
+        scratch_shapes=[
+            pltpu.VMEM((factors, every, BS), bf16),
+            pltpu.VMEM((factors, BS, width), bf16),
+            pltpu.VMEM((every, width), bf16),
+            pltpu.VMEM((every, width), bf16),
+            pltpu.VMEM((factors * BS, width), bf16),
+            pltpu.VMEM((every, BS), f32),
+            pltpu.VMEM((near, every, BS), bf16),
+            pltpu.VMEM((near, every, BS), bf16),
+            pltpu.VMEM((every, BS), bf16),
+            pltpu.VMEM((every, BS), bf16),
+            pltpu.VMEM((factors, BS, width), bf16),
+        ]
+        + [dma((groups,))] * 8
+        + [dma((near, groups))] * 4
+        + [dma((groups,))] * 6
+        + [dma((4,))],
+        compiler_params=pltpu.CompilerParams(
+            collective_id=0, has_side_effects=True, vmem_limit_bytes=50 * 2**20
+        ),
+        cost_estimate=pl.CostEstimate(flops=flops, bytes_accessed=8 * 2**20, transcendentals=every * width),
+    )(tokens, hidden_grad, w_up, pattern)
+    input_grad = (sums[0].astype(f32) + sums[1].astype(f32)).astype(bf16)
+    return (input_grad, grads.astype(f32))
+
+
+def body(tokens, hidden_grad, w_up, pattern):
+    groups, flies, factors = lax.axis_size("dp"), lax.axis_size("fly"), w_up.shape[0]
+    top = stride_of(factors - 1)
+    if groups * BS == tokens.shape[1] and groups > 1 and groups <= top < groups * flies:
+        return body_by_group(tokens, hidden_grad, w_up, pattern)
+    return body_general(tokens, hidden_grad, w_up, pattern)
+
+
 def solution(mesh):
     return jax.shard_map(
         body,

time: 894 us -> 150 us (0.17)
  waiting for transfers between devices: 663 us -> 0 us
  Pallas kernels: 0 us -> 142 us
  local copies, waits for them, and re-layouts: 128 us -> 3.61 us
  other arithmetic: 44.8 us -> 2.94 us
  matrix products: 36.7 us -> 0 us
  between operations: 14.4 us -> 0.66 us
    ppermute x11 -> x0, waiting for transfers between devices: 495 us -> none  [the longest x7 495 us: shifted(): lax.ppermute(value, axis, [(i, (i + by) % devices) for i in range(devices)])]
    all_gather x1 -> x0, waiting for transfers between devices: 167 us -> none  [body(): weights = lax.all_gather(w_up, 'dp', axis=1, tiled=True)]
    pallas_call x0 -> x1, Pallas kernels: none -> 142 us  [body_by_group(): pl.pallas_call(functools.partial(group_kernel, groups, flies), out_shape=...]
    dot_general x18 -> x0, matrix products: 36.7 us -> none  [the longest x6 18.2 us: body(): jnp.einsum('ngb,ngc->bgc', gathered[factor], grad_pre, preferred_element_...]
    transpose x6 -> x0, local copies, waits for them, and re-layouts: 33.4 us -> none  [body(): jnp.einsum('ngb,ngc->bgc', gathered[factor], grad_pre, preferred_element_...]
    reshape x6 -> x0, local copies, waits for them, and re-layouts: 29.9 us -> none  [body(): product_term.reshape(BS, hidden_width) * keep_f[factor][None, :]]
    add x7 -> x0, other arithmetic: 27.2 us -> none  [turn_one(): shifted(carry, 'dp', 1)]
    slice x8 -> x0, local copies, waits for them, and re-layouts: 26.1 us -> none  [the longest x7 26.1 us: body(): masked[factor]]
  transfers between devices with their start and end apart: 12 -> 0, of which waited for: 8 -> 0; matrix products, arithmetic and copies ran while one was open for 18% -> 0% of each run, Pallas kernels for 0% -> 0%
where the time goes in v2:
time: 150 us
  Pallas kernels  142 us (95%)
  local copies, waits for them, and re-layouts  3.61 us (2%)
  other arithmetic  2.94 us (2%)
    pallas_call x1, Pallas kernels, body_by_group(): pl.pallas_call(functools.partial(group_kernel, groups, flies), out_shape=...  142 us
    unnamed x8, local copies, waits for them, and re-layouts  3.61 us

profile of v2, /device:TPU:0, one launch (start us, length us, event | category | flops | bytes accessed | tf_op | source)
XLA Modules:
  0.0 149.7 jit_solution(9806973602711660579)
XLA Ops:
  0.6 0.0 copy-start
  0.6 1.2 copy-done
  1.9 0.0 copy-start.1
  1.9 1.0 copy-done.1
  2.9 0.0 copy-start.2
  2.9 0.7 copy-done.2
  3.6 142.5 %shard_map.59 = (bf16[2,128,2048]{2,1,0:T(8,128)(2,1)S(1)}, bf16[6,32,4096]{2,1,0:T(8,128)(2,1)}) custom-call(bf16[128,2048]{1,0:T(8,128)(2,1)S(1)} %copy-done.1, bf16[128,4096]{1,0:T(8,128)(2,1)S(1)} %copy-done, bf16[6,32,4096]{2,1,0:T(8,128)(2,1)} %w_up.1, s32[6,16]{1,0:T(8,128)S(1)} %copy-done.2), custom_call_target="tpu_custom_call" | custom-call | flops 4831838208 | bytes 8388608 | tf_op jit(solution)/shard_map/pallas_call | solution.py:330
  146.1 0.0 copy-start.3
  146.1 0.9 fusion
  147.0 0.7 copy-done.3
  147.7 2.0 %convert_element_type.21 = f32[6,32,4096]{2,1,0:T(8,128)} convert(bf16[6,32,4096]{2,1,0:T(8,128)(2,1)S(1)} %copy-done.3) | non-fusion elementwise | flops 786432 | bytes 4718592 | tf_op jit(solution)/shard_map/convert_element_type | solution.py:361
Async XLA Ops:
  0.6 1.2 copy-start
  1.9 1.0 copy-start.1
  2.9 0.7 copy-start.2
  146.1 1.6 %copy-start.3 = (bf16[6,32,4096]{2,1,0:T(8,128)(2,1)S(1)}, bf16[6,32,4096]{2,1,0:T(8,128)(2,1)}, u32[]{:S(2)}) copy-start(bf16[6,32,4096]{2,1,0:T(8,128)(2,1)} %get-tuple-element.5) | copy-start | bytes 4718596

commit v3 on v2

--- a/solution.py
+++ b/solution.py
@@ -125,7 +125,7 @@
 
 def group_kernel(
     groups, flies, tokens, hidden_grad, w_up, pattern, sums_out, grads_out,
-    feat, weights, upstream, grad_pre, masked, own_term, near_out, near_in, far_out, home_sum, product,
+    feat, weights, upstream, masked, own_term, near_out, near_in, far_out, home_sum, running, product,
     token_send, token_recv, far_send, far_recv, weight_send, weight_recv, up_send, up_recv,
     pass_send, pass_recv, back_send, back_recv, other_send, other_recv, home_send, home_recv,
     grad_send, grad_recv, local_sem,
@@ -172,7 +172,7 @@
         return remote(feat.at[0, part(s, rows)], feat.at[t, part(s, rows)], pass_send.at[i, s], pass_recv.at[i, s], partner(t))
 
     def back_copy(i, s):
-        return remote(near_out.at[i, part(s, rows)], near_in.at[i, part(s, rows)], back_send.at[i, s], back_recv.at[i, s], partner(near[i]))
+        return remote(near_out.at[i, part(s, 2 * rows)], near_in.at[i, part(s, 2 * rows)], back_send.at[i, s], back_recv.at[i, s], partner(near[i]))
 
     def other_copy(to, at):
         block = flipped(at, jnp.int32(half), groups)
@@ -181,8 +181,8 @@
     def home_copy(to, at):
         return remote(home_sum.at[part(to, rows)], sums_out.at[0, :, part(at, BS)], home_send.at[to], home_recv.at[at], {"dp": to})
 
-    def grad_copy(to, at):
-        return remote(product.at[:, part(to, share)], grads_out.at[:, :, part(at, width)], grad_send.at[to], grad_recv.at[at], {"dp": to})
+    def grad_copy(t, to, at):
+        return remote(product.at[t, part(to, share)], grads_out.at[t, :, part(at, width)], grad_send.at[t, to], grad_recv.at[t, at], {"dp": to})
 
     barrier = pltpu.get_barrier_semaphore()
     for k in range(1, groups):
@@ -193,7 +193,7 @@
     pl.semaphore_wait(barrier, groups - 1 + len(across))
 
     order = list(range(groups - 1, 0, -1))
-    for copy in (token_copy, far_copy, weight_copy, up_copy):
+    for copy in (token_copy, far_copy, weight_copy):
         for k in order:
             copy(peer(k), me).start()
     across_me = flipped(me, jnp.int32(half), groups)
@@ -218,6 +218,9 @@
         return carry
 
     lax.fori_loop(1, groups, pass_on, 0)
+    for k in order:
+        weight_copy(peer(k), me).wait_send()
+        up_copy(peer(k), me).start()
 
     place = lax.broadcasted_iota(jnp.int32, pattern.shape, 1)
     keep = [
@@ -233,72 +236,78 @@
             piece = weights[t, :, j * BS : (j + 1) * BS]
             masked[t * BS : (t + 1) * BS, j * BS : (j + 1) * BS] = piece * keep[j][t : t + 1].astype(jnp.bfloat16)
 
-    def work(source):
-        at = part(source, rows)
-        for i in range(len(near)):
-            pass_copy(i, source).wait_recv()
+    def sources(u):
+        return [peer(2 * u), peer(2 * u + 1)]
+
+    def pair(u):
+        return lax.div(peer(2 * u), jnp.int32(2))
+
+    def send_terms(u, rounded):
+        at = part(pair(u), 2 * rows)
+        contrib = lax.dot_general(rounded, masked[...], (((1,), (1,)), ((), ())), preferred_element_type=jnp.float32)
+        own_term[at, :] = contrib[:, :BS]
+        for i, t in enumerate(near):
+            near_out[i, at, :] = contrib[:, t * BS : (t + 1) * BS].astype(jnp.bfloat16)
+            back_copy(i, pair(u)).start()
+        far_out[at, :] = contrib[:, far * BS : (far + 1) * BS].astype(jnp.bfloat16)
+        for source in sources(u)[u == 0 :]:
+            other_copy(source, me).start()
+
+    pairs = groups // 2
+    for u in range(pairs):
+        at = part(pair(u), 2 * rows)
+        for source in sources(u):
+            for i in range(len(near)):
+                pass_copy(i, source).wait_recv()
+        for source in sources(u)[u == 0 :]:
+            far_copy(source, source).wait_recv()
+            up_copy(source, source).wait_recv()
         features = jnp.concatenate([feat[t, at, :] for t in range(factors)], axis=1)
         pre_act = jnp.dot(features, masked[...], preferred_element_type=jnp.float32)
         squash = jax.nn.sigmoid(pre_act)
         derivative = squash * (1.0 + pre_act * (1.0 - squash))
         rounded = (upstream[at, :].astype(jnp.float32) * derivative).astype(jnp.bfloat16)
-        grad_pre[at, :] = rounded
-        contrib = lax.dot_general(rounded, masked[...], (((1,), (1,)), ((), ())), preferred_element_type=jnp.float32)
-        own_term[at, :] = contrib[:, :BS]
-        far_out[at, :] = contrib[:, far * BS : (far + 1) * BS].astype(jnp.bfloat16)
-        for i, t in enumerate(near):
-            near_out[i, at, :] = contrib[:, t * BS : (t + 1) * BS].astype(jnp.bfloat16)
-            back_copy(i, source).start()
-
-    work(me)
+        if u < pairs - 1:
+            send_terms(u, rounded)
+        for t in range(factors):
+            term = lax.dot_general(feat[t, at, :], rounded, (((0,), (0,)), ((), ())), preferred_element_type=jnp.float32)
+            if u > 0:
+                term = running[t] + term
+            if u < pairs - 1:
+                running[t] = term
+                continue
+            for j in range(per_group):
+                scale = keep[j][t : t + 1] * (1.0 / groups)
+                product[t, :, j * BS : (j + 1) * BS] = (term[:, j * BS : (j + 1) * BS] * scale).astype(jnp.bfloat16)
+            for k in order:
+                grad_copy(t, peer(k), me).start()
+        if u == pairs - 1:
+            send_terms(u, rounded)
     own_far = pltpu.make_async_copy(far_out.at[part(me, rows)], sums_out.at[1, :, part(across_me, BS)], local_sem.at[1])
     own_far.start()
-
-    def work_step(k, carry):
-        source = flipped(me, k, groups)
-        far_copy(source, source).wait_recv()
-        up_copy(source, source).wait_recv()
-        work(source)
-        other_copy(source, me).start()
-        return carry
-
-    lax.fori_loop(1, groups, work_step, 0)
-
-    for t in range(factors):
-        term = lax.dot_general(feat[t], grad_pre[...], (((0,), (0,)), ((), ())), preferred_element_type=jnp.float32)
-        for j in range(per_group):
-            scale = keep[j][t : t + 1] * (1.0 / groups)
-            product[t, :, j * BS : (j + 1) * BS] = (term[:, j * BS : (j + 1) * BS] * scale).astype(jnp.bfloat16)
-    for k in order:
-        grad_copy(peer(k), me).start()
     own_grad = pltpu.make_async_copy(product.at[:, part(me, share)], grads_out.at[:, :, part(me, width)], local_sem.at[2])
     own_grad.start()
 
-    def add_up(source):
-        at = part(source, rows)
+    for u in range(pairs):
+        at = part(pair(u), 2 * rows)
         total = own_term[at, :]
         for i in range(len(near)):
-            back_copy(i, source).wait_recv()
+            back_copy(i, pair(u)).wait_recv()
             total = total + near_in[i, at, :].astype(jnp.float32)
         home_sum[at, :] = total.astype(jnp.bfloat16)
-
-    add_up(me)
+        for source in sources(u)[u == 0 :]:
+            home_copy(source, me).start()
     own_home = pltpu.make_async_copy(home_sum.at[part(me, rows)], sums_out.at[0, :, part(me, BS)], local_sem.at[0])
     own_home.start()
 
-    def add_step(k, carry):
-        source = flipped(me, k, groups)
-        add_up(source)
-        home_copy(source, me).start()
-        return carry
-
-    lax.fori_loop(1, groups, add_step, 0)
-
     def finish(k, carry):
         other = flipped(me, k, groups)
-        for copy in (other_copy, home_copy, grad_copy):
+        for copy in (other_copy, home_copy):
             copy(other, other).wait_recv()
-        for copy in (token_copy, far_copy, weight_copy, up_copy, other_copy, home_copy, grad_copy):
+        for t in range(factors):
+            grad_copy(t, other, other).wait_recv()
+            grad_copy(t, other, me).wait_send()
+        for copy in (token_copy, far_copy, up_copy, other_copy, home_copy):
             copy(other, me).wait_send()
         return carry
 
@@ -307,10 +316,12 @@
     def finish_near(s, carry):
         for i in range(len(near)):
             pass_copy(i, s).wait_send()
-            back_copy(i, s).wait_send()
         return carry
 
     lax.fori_loop(0, groups, finish_near, 0)
+    for u in range(pairs):
+        for i in range(len(near)):
+            back_copy(i, jnp.int32(u)).wait_send()
     own_far.wait()
     own_home.wait()
     own_grad.wait()
@@ -325,7 +336,7 @@
     near = factors - 2
     dma = pltpu.SemaphoreType.DMA
     bf16, f32 = jnp.bfloat16, jnp.float32
-    anywhere = pl.BlockSpec(memory_space=pl.ANY)
+    anywhere = pl.BlockSpec(memory_space=pltpu.HBM)
     flops = 6 * every * factors * BS * width
     sums, grads = pl.pallas_call(
         functools.partial(group_kernel, groups, flies),
@@ -339,21 +350,23 @@
             pltpu.VMEM((factors, every, BS), bf16),
             pltpu.VMEM((factors, BS, width), bf16),
             pltpu.VMEM((every, width), bf16),
-            pltpu.VMEM((every, width), bf16),
             pltpu.VMEM((factors * BS, width), bf16),
             pltpu.VMEM((every, BS), f32),
             pltpu.VMEM((near, every, BS), bf16),
             pltpu.VMEM((near, every, BS), bf16),
             pltpu.VMEM((every, BS), bf16),
             pltpu.VMEM((every, BS), bf16),
+            pltpu.VMEM((factors, BS, width), f32),
             pltpu.VMEM((factors, BS, width), bf16),
         ]
         + [dma((groups,))] * 8
-        + [dma((near, groups))] * 4
-        + [dma((groups,))] * 6
+        + [dma((near, groups))] * 2
+        + [dma((near, groups // 2))] * 2
+        + [dma((groups,))] * 4
+        + [dma((factors, groups))] * 2
         + [dma((4,))],
         compiler_params=pltpu.CompilerParams(
-            collective_id=0, has_side_effects=True, vmem_limit_bytes=50 * 2**20
+            collective_id=0, has_side_effects=True, vmem_limit_bytes=63 * 2**20
         ),
         cost_estimate=pl.CostEstimate(flops=flops, bytes_accessed=8 * 2**20, transcendentals=every * width),
     )(tokens, hidden_grad, w_up, pattern)
@@ -364,7 +377,7 @@
 def body(tokens, hidden_grad, w_up, pattern):
     groups, flies, factors = lax.axis_size("dp"), lax.axis_size("fly"), w_up.shape[0]
     top = stride_of(factors - 1)
-    if groups * BS == tokens.shape[1] and groups > 1 and groups <= top < groups * flies:
+    if groups * BS == tokens.shape[1] and groups > 1 and groups & (groups - 1) == 0 and groups <= top < groups * flies:
         return body_by_group(tokens, hidden_grad, w_up, pattern)
     return body_general(tokens, hidden_grad, w_up, pattern)
 

time: 150 us -> 151 us (level)
  Pallas kernels: 142 us -> 146 us
  local copies, waits for them, and re-layouts: 3.61 us -> 0.01 us
    unnamed x8 -> x2, local copies, waits for them, and re-layouts: 3.61 us -> 0.01 us
    pallas_call x1, Pallas kernels: 142 us -> 146 us  [body_by_group(): pl.pallas_call(functools.partial(group_kernel, groups, flies), out_shape=...]
where the time goes in v3:
time: 151 us
  Pallas kernels  146 us (97%)
  other arithmetic  4.26 us (3%)
    pallas_call x1, Pallas kernels, body_by_group(): pl.pallas_call(functools.partial(group_kernel, groups, flies), out_shape=...  146 us

profile of v3, /device:TPU:0, one launch (start us, length us, event | category | flops | bytes accessed | tf_op | source)
XLA Modules:
  0.0 150.7 jit_solution(13426315758940963328)
XLA Ops:
  0.6 145.8 %shard_map.59 = (bf16[2,128,2048]{2,1,0:T(8,128)(2,1)}, bf16[6,32,4096]{2,1,0:T(8,128)(2,1)}) custom-call(bf16[128,2048]{1,0:T(8,128)(2,1)} %tokens.1, bf16[128,4096]{1,0:T(8,128)(2,1)} %hidden_grad.1, bf16[6,32,4096]{2,1,0:T(8,128)(2,1)} %w_up.1, s32[6,16]{1,0:T(8,128)} %pattern.1), custom_call_target="tpu_custom_call" | custom-call | flops 4831838208 | bytes 8388608 | tf_op jit(solution)/shard_map/pallas_call | solution.py:341
  146.4 0.0 copy-start
  146.4 2.2 %fusion = bf16[128,2048]{1,0:T(8,128)(2,1)} fusion(bf16[2,128,2048]{2,1,0:T(8,128)(2,1)} %get-tuple-element.4), kind=kLoop, calls=%fused_computation.1 | loop fusion | flops 1048576 | bytes 1572864 | tf_op jit(solution)/shard_map/convert_element_type | solution.py:373
  148.7 0.0 copy-done
  148.7 2.0 %convert_element_type.21 = f32[6,32,4096]{2,1,0:T(8,128)} convert(bf16[6,32,4096]{2,1,0:T(8,128)(2,1)S(1)} %copy-done) | non-fusion elementwise | flops 786432 | bytes 4718592 | tf_op jit(solution)/shard_map/convert_element_type | solution.py:374
Async XLA Ops:
  146.4 2.3 %copy-start = (bf16[6,32,4096]{2,1,0:T(8,128)(2,1)S(1)}, bf16[6,32,4096]{2,1,0:T(8,128)(2,1)}, u32[]{:S(2)}) copy-start(bf16[6,32,4096]{2,1,0:T(8,128)(2,1)} %get-tuple-element.5) | copy-start | bytes 4718596

commit v4 on v3

--- a/solution.py
+++ b/solution.py
@@ -192,10 +192,14 @@
         pl.semaphore_signal(barrier, inc=1, device_id=partner(t), device_id_type=pl.DeviceIdType.MESH)
     pl.semaphore_wait(barrier, groups - 1 + len(across))
 
-    order = list(range(groups - 1, 0, -1))
-    for copy in (token_copy, far_copy, weight_copy):
-        for k in order:
-            copy(peer(k), me).start()
+    order = []
+    for k in range(half):
+        order += [groups - 1 - k] + ([k + 1] if k + 1 < half else [])
+    for k in order:
+        token_copy(peer(k), me).start()
+        far_copy(peer(k), me).start()
+    for k in order:
+        weight_copy(peer(k), me).start()
     across_me = flipped(me, jnp.int32(half), groups)
     local = [
         pltpu.make_async_copy(tokens.at[:, part(me, BS)], feat.at[0, part(me, rows)], local_sem.at[0]),
@@ -210,16 +214,11 @@
     for i in range(len(near)):
         pass_copy(i, me).start()
 
-    def pass_on(k, carry):
-        source = flipped(me, k, groups)
-        token_copy(source, source).wait_recv()
+    for k in order:
+        token_copy(peer(k), peer(k)).wait_recv()
         for i in range(len(near)):
-            pass_copy(i, source).start()
-        return carry
-
-    lax.fori_loop(1, groups, pass_on, 0)
+            pass_copy(i, peer(k)).start()
     for k in order:
-        weight_copy(peer(k), me).wait_send()
         up_copy(peer(k), me).start()
 
     place = lax.broadcasted_iota(jnp.int32, pattern.shape, 1)
@@ -307,7 +306,7 @@
         for t in range(factors):
             grad_copy(t, other, other).wait_recv()
             grad_copy(t, other, me).wait_send()
-        for copy in (token_copy, far_copy, up_copy, other_copy, home_copy):
+        for copy in (token_copy, far_copy, weight_copy, up_copy, other_copy, home_copy):
             copy(other, me).wait_send()
         return carry
 

time: 151 us -> 152 us (level)
  no operation moved by 1% of the time
where the time goes in v4:
time: 152 us; the launch traced here: 151 us
  Pallas kernels  146 us (96%)
  other arithmetic  4.26 us (3%)
    pallas_call x1, Pallas kernels, body_by_group(): pl.pallas_call(functools.partial(group_kernel, groups, flies), out_shape=...  146 us

profile of v4, /device:TPU:0, one launch (start us, length us, event | category | flops | bytes accessed | tf_op | source)
XLA Modules:
  0.0 150.8 jit_solution(14513294389575189099)
XLA Ops:
  0.6 145.9 %shard_map.59 = (bf16[2,128,2048]{2,1,0:T(8,128)(2,1)}, bf16[6,32,4096]{2,1,0:T(8,128)(2,1)}) custom-call(bf16[128,2048]{1,0:T(8,128)(2,1)} %tokens.1, bf16[128,4096]{1,0:T(8,128)(2,1)} %hidden_grad.1, bf16[6,32,4096]{2,1,0:T(8,128)(2,1)} %w_up.1, s32[6,16]{1,0:T(8,128)} %pattern.1), custom_call_target="tpu_custom_call" | custom-call | flops 4831838208 | bytes 8388608 | tf_op jit(solution)/shard_map/pallas_call | solution.py:340
  146.5 0.0 copy-start
  146.5 2.2 %fusion = bf16[128,2048]{1,0:T(8,128)(2,1)} fusion(bf16[2,128,2048]{2,1,0:T(8,128)(2,1)} %get-tuple-element.4), kind=kLoop, calls=%fused_computation.1 | loop fusion | flops 1048576 | bytes 1572864 | tf_op jit(solution)/shard_map/convert_element_type | solution.py:372
  148.8 0.0 copy-done
  148.8 2.0 %convert_element_type.21 = f32[6,32,4096]{2,1,0:T(8,128)} convert(bf16[6,32,4096]{2,1,0:T(8,128)(2,1)S(1)} %copy-done) | non-fusion elementwise | flops 786432 | bytes 4718592 | tf_op jit(solution)/shard_map/convert_element_type | solution.py:373
Async XLA Ops:
  146.5 2.3 %copy-start = (bf16[6,32,4096]{2,1,0:T(8,128)(2,1)S(1)}, bf16[6,32,4096]{2,1,0:T(8,128)(2,1)}, u32[]{:S(2)}) copy-start(bf16[6,32,4096]{2,1,0:T(8,128)(2,1)} %get-tuple-element.5) | copy-start | bytes 4718596

commit v5 on v3

--- a/solution.py
+++ b/solution.py
@@ -125,7 +125,7 @@
 
 def group_kernel(
     groups, flies, tokens, hidden_grad, w_up, pattern, sums_out, grads_out,
-    feat, weights, upstream, masked, own_term, near_out, near_in, far_out, home_sum, running, product,
+    feat, weights, upstream, masked, own_term, near_out, near_in, far_out, home_sum, slope, grad_pre, product,
     token_send, token_recv, far_send, far_recv, weight_send, weight_recv, up_send, up_recv,
     pass_send, pass_recv, back_send, back_recv, other_send, other_recv, home_send, home_recv,
     grad_send, grad_recv, local_sem,
@@ -242,9 +242,9 @@
     def pair(u):
         return lax.div(peer(2 * u), jnp.int32(2))
 
-    def send_terms(u, rounded):
+    def send_terms(u):
         at = part(pair(u), 2 * rows)
-        contrib = lax.dot_general(rounded, masked[...], (((1,), (1,)), ((), ())), preferred_element_type=jnp.float32)
+        contrib = lax.dot_general(grad_pre[at, :], masked[...], (((1,), (1,)), ((), ())), preferred_element_type=jnp.float32)
         own_term[at, :] = contrib[:, :BS]
         for i, t in enumerate(near):
             near_out[i, at, :] = contrib[:, t * BS : (t + 1) * BS].astype(jnp.bfloat16)
@@ -261,28 +261,24 @@
                 pass_copy(i, source).wait_recv()
         for source in sources(u)[u == 0 :]:
             far_copy(source, source).wait_recv()
-            up_copy(source, source).wait_recv()
         features = jnp.concatenate([feat[t, at, :] for t in range(factors)], axis=1)
         pre_act = jnp.dot(features, masked[...], preferred_element_type=jnp.float32)
         squash = jax.nn.sigmoid(pre_act)
-        derivative = squash * (1.0 + pre_act * (1.0 - squash))
-        rounded = (upstream[at, :].astype(jnp.float32) * derivative).astype(jnp.bfloat16)
-        if u < pairs - 1:
-            send_terms(u, rounded)
-        for t in range(factors):
-            term = lax.dot_general(feat[t, at, :], rounded, (((0,), (0,)), ((), ())), preferred_element_type=jnp.float32)
-            if u > 0:
-                term = running[t] + term
-            if u < pairs - 1:
-                running[t] = term
-                continue
-            for j in range(per_group):
-                scale = keep[j][t : t + 1] * (1.0 / groups)
-                product[t, :, j * BS : (j + 1) * BS] = (term[:, j * BS : (j + 1) * BS] * scale).astype(jnp.bfloat16)
-            for k in order:
-                grad_copy(t, peer(k), me).start()
-        if u == pairs - 1:
-            send_terms(u, rounded)
+        slope[at, :] = squash * (1.0 + pre_act * (1.0 - squash))
+    for u in range(pairs):
+        at = part(pair(u), 2 * rows)
+        for source in sources(u)[u == 0 :]:
+            up_copy(source, source).wait_recv()
+        grad_pre[at, :] = (upstream[at, :].astype(jnp.float32) * slope[at, :]).astype(jnp.bfloat16)
+    for t in range(factors):
+        term = lax.dot_general(feat[t], grad_pre[...], (((0,), (0,)), ((), ())), preferred_element_type=jnp.float32)
+        for j in range(per_group):
+            scale = keep[j][t : t + 1] * (1.0 / groups)
+            product[t, :, j * BS : (j + 1) * BS] = (term[:, j * BS : (j + 1) * BS] * scale).astype(jnp.bfloat16)
+        for k in order:
+            grad_copy(t, peer(k), me).start()
+    for u in range(pairs):
+        send_terms(u)
     own_far = pltpu.make_async_copy(far_out.at[part(me, rows)], sums_out.at[1, :, part(across_me, BS)], local_sem.at[1])
     own_far.start()
     own_grad = pltpu.make_async_copy(product.at[:, part(me, share)], grads_out.at[:, :, part(me, width)], local_sem.at[2])
@@ -356,7 +352,8 @@
             pltpu.VMEM((near, every, BS), bf16),
             pltpu.VMEM((every, BS), bf16),
             pltpu.VMEM((every, BS), bf16),
-            pltpu.VMEM((factors, BS, width), f32),
+            pltpu.VMEM((every, width), f32),
+            pltpu.VMEM((every, width), bf16),
             pltpu.VMEM((factors, BS, width), bf16),
         ]
         + [dma((groups,))] * 8

time: 151 us -> 152 us (level)
  no operation moved by 1% of the time
where the time goes in v5:
time: 152 us; the launch traced here: 151 us
  Pallas kernels  146 us (96%)
  other arithmetic  4.26 us (3%)
    pallas_call x1, Pallas kernels, body_by_group(): pl.pallas_call(functools.partial(group_kernel, groups, flies), out_shape=...  146 us

profile of v5, /device:TPU:0, one launch (start us, length us, event | category | flops | bytes accessed | tf_op | source)
XLA Modules:
  0.0 150.8 jit_solution(6313353802401914615)
XLA Ops:
  0.6 145.9 %shard_map.59 = (bf16[2,128,2048]{2,1,0:T(8,128)(2,1)}, bf16[6,32,4096]{2,1,0:T(8,128)(2,1)}) custom-call(bf16[128,2048]{1,0:T(8,128)(2,1)} %tokens.1, bf16[128,4096]{1,0:T(8,128)(2,1)} %hidden_grad.1, bf16[6,32,4096]{2,1,0:T(8,128)(2,1)} %w_up.1, s32[6,16]{1,0:T(8,128)} %pattern.1), custom_call_target="tpu_custom_call" | custom-call | flops 4831838208 | bytes 8388608 | tf_op jit(solution)/shard_map/pallas_call | solution.py:337
  146.5 0.0 copy-start
  146.5 2.2 %fusion = bf16[128,2048]{1,0:T(8,128)(2,1)} fusion(bf16[2,128,2048]{2,1,0:T(8,128)(2,1)} %get-tuple-element.4), kind=kLoop, calls=%fused_computation.1 | loop fusion | flops 1048576 | bytes 1572864 | tf_op jit(solution)/shard_map/convert_element_type | solution.py:370
  148.8 0.0 copy-done
  148.8 2.0 %convert_element_type.21 = f32[6,32,4096]{2,1,0:T(8,128)} convert(bf16[6,32,4096]{2,1,0:T(8,128)(2,1)S(1)} %copy-done) | non-fusion elementwise | flops 786432 | bytes 4718592 | tf_op jit(solution)/shard_map/convert_element_type | solution.py:371
Async XLA Ops:
  146.5 2.3 %copy-start = (bf16[6,32,4096]{2,1,0:T(8,128)(2,1)S(1)}, bf16[6,32,4096]{2,1,0:T(8,128)(2,1)}, u32[]{:S(2)}) copy-start(bf16[6,32,4096]{2,1,0:T(8,128)(2,1)} %get-tuple-element.5) | copy-start | bytes 4718596

commit v6 on v5

--- a/solution.py
+++ b/solution.py
@@ -181,8 +181,8 @@
     def home_copy(to, at):
         return remote(home_sum.at[part(to, rows)], sums_out.at[0, :, part(at, BS)], home_send.at[to], home_recv.at[at], {"dp": to})
 
-    def grad_copy(t, to, at):
-        return remote(product.at[t, part(to, share)], grads_out.at[t, :, part(at, width)], grad_send.at[t, to], grad_recv.at[t, at], {"dp": to})
+    def grad_copy(to, at):
+        return remote(product.at[:, part(to, share)], grads_out.at[:, :, part(at, width)], grad_send.at[to], grad_recv.at[at], {"dp": to})
 
     barrier = pltpu.get_barrier_semaphore()
     for k in range(1, groups):
@@ -193,7 +193,7 @@
     pl.semaphore_wait(barrier, groups - 1 + len(across))
 
     order = list(range(groups - 1, 0, -1))
-    for copy in (token_copy, far_copy, weight_copy):
+    for copy in (token_copy, far_copy, weight_copy, up_copy):
         for k in order:
             copy(peer(k), me).start()
     across_me = flipped(me, jnp.int32(half), groups)
@@ -218,9 +218,6 @@
         return carry
 
     lax.fori_loop(1, groups, pass_on, 0)
-    for k in order:
-        weight_copy(peer(k), me).wait_send()
-        up_copy(peer(k), me).start()
 
     place = lax.broadcasted_iota(jnp.int32, pattern.shape, 1)
     keep = [
@@ -275,8 +272,8 @@
         for j in range(per_group):
             scale = keep[j][t : t + 1] * (1.0 / groups)
             product[t, :, j * BS : (j + 1) * BS] = (term[:, j * BS : (j + 1) * BS] * scale).astype(jnp.bfloat16)
-        for k in order:
-            grad_copy(t, peer(k), me).start()
+    for k in order:
+        grad_copy(peer(k), me).start()
     for u in range(pairs):
         send_terms(u)
     own_far = pltpu.make_async_copy(far_out.at[part(me, rows)], sums_out.at[1, :, part(across_me, BS)], local_sem.at[1])
@@ -298,12 +295,9 @@
 
     def finish(k, carry):
         other = flipped(me, k, groups)
-        for copy in (other_copy, home_copy):
+        for copy in (other_copy, home_copy, grad_copy):
             copy(other, other).wait_recv()
-        for t in range(factors):
-            grad_copy(t, other, other).wait_recv()
-            grad_copy(t, other, me).wait_send()
-        for copy in (token_copy, far_copy, up_copy, other_copy, home_copy):
+        for copy in (token_copy, far_copy, weight_copy, up_copy, other_copy, home_copy, grad_copy):
             copy(other, me).wait_send()
         return carry
 
@@ -332,7 +326,7 @@
     near = factors - 2
     dma = pltpu.SemaphoreType.DMA
     bf16, f32 = jnp.bfloat16, jnp.float32
-    anywhere = pl.BlockSpec(memory_space=pltpu.HBM)
+    anywhere = pl.BlockSpec(memory_space=pl.ANY)
     flops = 6 * every * factors * BS * width
     sums, grads = pl.pallas_call(
         functools.partial(group_kernel, groups, flies),
@@ -359,11 +353,10 @@
         + [dma((groups,))] * 8
         + [dma((near, groups))] * 2
         + [dma((near, groups // 2))] * 2
-        + [dma((groups,))] * 4
-        + [dma((factors, groups))] * 2
+        + [dma((groups,))] * 6
         + [dma((4,))],
         compiler_params=pltpu.CompilerParams(
-            collective_id=0, has_side_effects=True, vmem_limit_bytes=63 * 2**20
+            collective_id=0, has_side_effects=True, vmem_limit_bytes=50 * 2**20
         ),
         cost_estimate=pl.CostEstimate(flops=flops, bytes_accessed=8 * 2**20, transcendentals=every * width),
     )(tokens, hidden_grad, w_up, pattern)

time: 152 us -> 154 us (1.013)
  local copies, waits for them, and re-layouts: 0.01 us -> 3.61 us
    unnamed x2 -> x8, local copies, waits for them, and re-layouts: 0.01 us -> 3.61 us
where the time goes in v6:
time: 154 us; the launch traced here: 153 us
  Pallas kernels  145 us (94%)
  local copies, waits for them, and re-layouts  3.61 us (2%)
  other arithmetic  2.94 us (2%)
    pallas_call x1, Pallas kernels, body_by_group(): pl.pallas_call(functools.partial(group_kernel, groups, flies), out_shape=...  145 us
    unnamed x8, local copies, waits for them, and re-layouts  3.61 us

profile of v6, /device:TPU:0, one launch (start us, length us, event | category | flops | bytes accessed | tf_op | source)
XLA Modules:
  0.0 152.6 jit_solution(15564532686766104842)
XLA Ops:
  0.6 0.0 copy-start
  0.6 1.2 copy-done
  1.9 0.0 copy-start.1
  1.9 1.0 copy-done.1
  2.9 0.0 copy-start.2
  2.9 0.7 copy-done.2
  3.6 145.4 %shard_map.59 = (bf16[2,128,2048]{2,1,0:T(8,128)(2,1)S(1)}, bf16[6,32,4096]{2,1,0:T(8,128)(2,1)}) custom-call(bf16[128,2048]{1,0:T(8,128)(2,1)S(1)} %copy-done.1, bf16[128,4096]{1,0:T(8,128)(2,1)S(1)} %copy-done, bf16[6,32,4096]{2,1,0:T(8,128)(2,1)} %w_up.1, s32[6,16]{1,0:T(8,128)S(1)} %copy-done.2), custom_call_target="tpu_custom_call" | custom-call | flops 4831838208 | bytes 8388608 | tf_op jit(solution)/shard_map/pallas_call | solution.py:331
  149.0 0.0 copy-start.3
  149.0 0.9 fusion
  149.9 0.7 copy-done.3
  150.6 2.0 %convert_element_type.21 = f32[6,32,4096]{2,1,0:T(8,128)} convert(bf16[6,32,4096]{2,1,0:T(8,128)(2,1)S(1)} %copy-done.3) | non-fusion elementwise | flops 786432 | bytes 4718592 | tf_op jit(solution)/shard_map/convert_element_type | solution.py:364
Async XLA Ops:
  0.6 1.2 copy-start
  1.9 1.0 copy-start.1
  2.9 0.7 copy-start.2
  149.0 1.6 %copy-start.3 = (bf16[6,32,4096]{2,1,0:T(8,128)(2,1)S(1)}, bf16[6,32,4096]{2,1,0:T(8,128)(2,1)}, u32[]{:S(2)}) copy-start(bf16[6,32,4096]{2,1,0:T(8,128)(2,1)} %get-tuple-element.5) | copy-start | bytes 4718596
